TPU v7x, 256 devices: a whole 4x4x8 slice. The times are simulated.
256 devices in a mesh: prow: 16 (over z, core), pcol: 16 (over y, x).
Axes of the slice: x: 4, y: 4, z: 8, core: 2. Of those that a mesh axis runs over, the one named last changes fastest.
Arguments:
- matrix: float32 [16384, 24576], P('prow', 'pcol'), may hold values from -4 to 4, as said below
Outputs:
- factored: float32 [16384, 24576], P('prow', 'pcol')
- t_factor: float32 [128, 128], replicated
Inputs may be any that keep to these rules, and one draw needn't show every extreme that they name: `matrix`: the panel has full column rank, and the diagonal entries of the top 128 x 128 block of orthogonal are 0.4 or more.
All inputs are finite; a program needn't handle non-finite values.
Results may differ from a plain program's by a relative error of at most 0.0003.
Values sent between devices are 32-bit elements; how exact they have to be, the bound alone decides.
A program may use at most 64 MiB of HBM per device.

v0:
```python
import jax
import jax.numpy as jnp
from jax import lax
from jax.sharding import PartitionSpec as P

B = 128


def swapped(block, axis, apart):
    count = lax.axis_size(axis)
    route = []
    for low in range(count):
        high = low | 1 << apart
        if high != low and high < count:
            route += [(low, high), (high, low)]
    return lax.ppermute(block, axis, route)


def broadcast(value, axis, source):
    kept = jnp.where(lax.axis_index(axis) == source, value, 0).astype(value.dtype)
    return lax.psum(kept, axis)


def product(left, right):
    return jnp.dot(left, right, precision=lax.Precision.HIGHEST)


def pick_row(square, level):
    position = jnp.arange(square.shape[0])
    return jnp.sum(jnp.where((position == level)[:, None], square, 0.0), axis=0)


def pick_column(square, level):
    position = jnp.arange(square.shape[1])
    return jnp.sum(jnp.where((position == level)[None, :], square, 0.0), axis=1)


def pick_entry(vector, level):
    position = jnp.arange(vector.shape[0])
    return jnp.sum(jnp.where(position == level, vector, 0.0))


def cholesky_upper(gram_matrix):
    order = gram_matrix.shape[0]
    position = jnp.arange(order)

    def cholesky_advance(level, state):
        remain, lower = state
        column = pick_column(remain, level)
        pivot_value = jnp.sqrt(pick_entry(column, level))
        column = jnp.where(position >= level, column / pivot_value, 0.0)
        remain = remain - column[:, None] * column[None, :]
        lower = lower + jnp.where((position == level)[None, :], column[:, None], 0.0)
        return (remain, lower)

    start = (gram_matrix, jnp.zeros_like(gram_matrix))
    remain, lower = lax.fori_loop(0, order, cholesky_advance, start)
    return lower.T


def upper_inverse(upper):
    order = upper.shape[0]
    position = jnp.arange(order)

    def upper_advance(count, inverse):
        level = order - 1 - count
        row = pick_row(upper, level)
        pivot_value = pick_entry(row, level)
        beyond = jnp.where(position > level, row, 0.0)
        unit_row = jnp.where(position == level, 1.0, 0.0).astype(upper.dtype)
        new_row = (unit_row - product(beyond[None, :], inverse)[0]) / pivot_value
        return inverse + jnp.where((position == level)[:, None], new_row[None, :], 0.0)

    return lax.fori_loop(0, order, upper_advance, jnp.zeros_like(upper))


def unit_lower_inverse(lower):
    order = lower.shape[0]
    position = jnp.arange(order)

    def unit_advance(level, inverse):
        row = pick_row(lower, level)
        before = jnp.where(position < level, row, 0.0)
        unit_row = jnp.where(position == level, 1.0, 0.0).astype(lower.dtype)
        new_row = unit_row - product(before[None, :], inverse)[0]
        return inverse + jnp.where((position == level)[:, None], new_row[None, :], 0.0)

    return lax.fori_loop(0, order, unit_advance, jnp.zeros_like(lower))


def small_factors(square):
    order = square.shape[0]
    position = jnp.arange(order)

    def small_advance(level, packed):
        column_full = pick_column(packed, level)
        pivot_value = pick_entry(column_full, level)
        column = jnp.where(position > level, column_full / pivot_value, 0.0)
        pivot_row = jnp.where(position > level, pick_row(packed, level), 0.0)
        packed = packed - column[:, None] * pivot_row[None, :]
        fixed_column = jnp.where(position > level, column, column_full)
        return jnp.where((position == level)[None, :], fixed_column[:, None], packed)

    packed = lax.fori_loop(0, order, small_advance, square)
    return (jnp.tril(packed, -1) + jnp.eye(order, dtype=square.dtype), jnp.triu(packed))


def split_triangles(square):
    order = square.shape[0]
    width = min(order, 16)
    packed = square
    for start in range(0, order, width):
        finish = start + width
        lower_block, upper_block = small_factors(packed[start:finish, start:finish])
        packed = packed.at[start:finish, start:finish].set(jnp.tril(lower_block, -1) + upper_block)
        if finish < order:
            below = packed[finish:, start:finish]
            right = packed[start:finish, finish:]
            column_part = product(below, upper_inverse(upper_block))
            row_part = product(unit_lower_inverse(lower_block), right)
            packed = packed.at[finish:, start:finish].set(column_part)
            packed = packed.at[start:finish, finish:].set(row_part)
            packed = packed.at[finish:, finish:].set(
                packed[finish:, finish:] - product(column_part, row_part)
            )
    unit_lower = jnp.tril(packed, -1) + jnp.eye(order, dtype=square.dtype)
    return (unit_lower, jnp.triu(packed))


def inner_rows(left, right):
    return lax.dot_general(left, right, (((0,), (0,)), ((), ())), precision=lax.Precision.HIGHEST)


def per_device(matrix):
    rows_local = matrix.shape[0]
    row_index = lax.axis_index("prow")
    col_index = lax.axis_index("pcol")
    identity = jnp.eye(B, dtype=jnp.float32)
    panel_cols = matrix[:, :B]
    gram_local = inner_rows(panel_cols, panel_cols)
    factor_r = cholesky_upper(gram_local)
    for level in range(lax.axis_size("prow").bit_length() - 1):
        partner = swapped(factor_r, "prow", level)
        factor_r = cholesky_upper(inner_rows(factor_r, factor_r) + inner_rows(partner, partner))
    r_inverse = upper_inverse(factor_r)
    orthogonal = product(panel_cols, r_inverse)
    unit_lower, upper_part = split_triangles(orthogonal[:B] + identity)
    unit_lower, upper_part = (broadcast(unit_lower, "prow", 0), broadcast(upper_part, "prow", 0))
    part_inverse = upper_inverse(upper_part)
    lower_rows = product(orthogonal, part_inverse)
    position = jnp.arange(rows_local)[:, None]
    top_mask = jnp.logical_and(row_index == 0, position < B)
    filler = jnp.zeros((rows_local - B, B), jnp.float32)
    reflectors = jnp.where(top_mask, jnp.concatenate([unit_lower, filler], axis=0), lower_rows)
    t_factor = product(upper_part, unit_lower_inverse(unit_lower).T)
    reflectors, t_factor = (broadcast(reflectors, "pcol", 0), broadcast(t_factor, "pcol", 0))
    projected = lax.psum(inner_rows(reflectors, matrix), "prow")
    weights = product(t_factor.T, projected)
    updated = matrix - product(reflectors, weights)
    top_rows = jnp.triu(-factor_r) + jnp.tril(unit_lower, -1)
    panel_out = jnp.where(top_mask, jnp.concatenate([top_rows, filler], axis=0), reflectors)
    first_block = jnp.where(col_index == 0, panel_out, updated[:, :B])
    factored = jnp.concatenate([first_block, updated[:, B:]], axis=1)
    return (factored, t_factor)


def solution(mesh):
    return jax.shard_map(
        per_device,
        mesh=mesh,
        in_specs=(P("prow", "pcol"),),
        out_specs=(P("prow", "pcol"), P()),
        check_vma=False,
    )
```

profile of v0, /device:TPU:25, one launch (start us, length us, event | category | flops | bytes accessed | tf_op | source)
XLA Modules:
  0.0 2314.6 jit_solution(6715228317190640486)
XLA Ops:
  9.4 199.0 %while.497 = (s32[]{:T(128)}, f32[128,128]{1,0:T(8,128)S(1)}, f32[128,128]{1,0:T(8,128)S(1)}, s32[]{:T(128)}, s32[]{:T(128)}) while((s32[]{:T(128)}, f32[128,128]{1,0:T(8,128)S(1)}, f32[128,128]{1,0:T(8,128)S(1)}, s32[]{:T(128)}, s32[]{:T(128)}) %tuple.1130), condition=%wide.region_3.4_spmd.clone.clone, body=%wide.region_0.3_spmd.clone.clone.sunk | while | flops 115458 | bytes 330731 | solution.py:57
  211.9 200.0 %while.498 = (s32[]{:T(128)}, f32[128,128]{1,0:T(8,128)S(1)}, f32[128,128]{1,0:T(8,128)S(1)}, s32[]{:T(128)}, s32[]{:T(128)}) while((s32[]{:T(128)}, f32[128,128]{1,0:T(8,128)S(1)}, f32[128,128]{1,0:T(8,128)S(1)}, s32[]{:T(128)}, s32[]{:T(128)}) %tuple.1133), condition=%wide.region_7.8_spmd.clone.clone, body=%wide.region_4.7_spmd.clone.clone.sunk | while | flops 115458 | bytes 330731 | solution.py:57
  416.2 214.4 %while.499 = (s32[]{:T(128)}, f32[128,128]{1,0:T(8,128)S(1)}, f32[128,128]{1,0:T(8,128)S(1)}, s32[]{:T(128)}, s32[]{:T(128)}) while((s32[]{:T(128)}, f32[128,128]{1,0:T(8,128)S(1)}, f32[128,128]{1,0:T(8,128)S(1)}, s32[]{:T(128)}, s32[]{:T(128)}) %tuple.1136), condition=%wide.region_11.12_spmd.clone.clone, body=%wide.region_8.11_spmd.clone.clone.sunk | while | flops 115458 | bytes 330731 | solution.py:57
  635.7 210.5 %while.500 = (s32[]{:T(128)}, f32[128,128]{1,0:T(8,128)S(1)}, f32[128,128]{1,0:T(8,128)S(1)}, s32[]{:T(128)}, s32[]{:T(128)}) while((s32[]{:T(128)}, f32[128,128]{1,0:T(8,128)S(1)}, f32[128,128]{1,0:T(8,128)S(1)}, s32[]{:T(128)}, s32[]{:T(128)}) %tuple.1139), condition=%wide.region_15.16_spmd.clone.clone, body=%wide.region_12.15_spmd.clone.clone.sunk | while | flops 115458 | bytes 330731 | solution.py:57
  855.4 189.8 %while.501 = (s32[]{:T(128)}, f32[128,128]{1,0:T(8,128)S(1)}, f32[128,128]{1,0:T(8,128)S(1)}, s32[]{:T(128)}, s32[]{:T(128)}) while((s32[]{:T(128)}, f32[128,128]{1,0:T(8,128)S(1)}, f32[128,128]{1,0:T(8,128)S(1)}, s32[]{:T(128)}, s32[]{:T(128)}) %tuple.1142), condition=%wide.region_19.20_spmd.clone.clone, body=%wide.region_16.19_spmd.clone.clone.sunk | while | flops 115458 | bytes 330731 | solution.py:57
  1045.2 211.7 %while.502 = (s32[]{:T(128)}, f32[128,128]{1,0:T(8,128)S(1)}, f32[128,128]{1,0:T(8,128)S(1)}, s32[]{:T(128)}, s32[]{:T(128)}, /*index=5*/s32[]{:T(128)}) while((s32[]{:T(128)}, f32[128,128]{1,0:T(8,128)S(1)}, f32[128,128]{1,0:T(8,128)S(1)}, s32[]{:T(128)}, s32[]{:T(128)}, /*index=5*/s32[]{:T(128)}) %tuple.1145), condition=%wide.region_23.24_spmd.clone.clone, body=%wide.region_20.23_spmd.clone.clone.sunk | while | flops 296067 | bytes 265208 | solution.py:74
  1258.7 23.5 %while.489 = (s32[]{:T(128)}, f32[16,16]{1,0:T(8,128)S(1)}, s32[]{:T(128)}) while((s32[]{:T(128)}, f32[16,16]{1,0:T(8,128)S(1)}, s32[]{:T(128)}) %tuple.1148), condition=%wide.region_28.29_spmd.clone.clone, body=%wide.region_24.28_spmd.clone.clone.sunk | while | flops 1905 | bytes 3897 | solution.py:104
  1288.0 25.0 %while.503 = (s32[]{:T(128)}, f32[16,16]{1,0:T(8,128)S(1)}, f32[16,16]{1,0:T(8,128)S(1)}, s32[]{:T(128)}, s32[]{:T(128)}, /*index=5*/s32[]{:T(128)}) while((s32[]{:T(128)}, f32[16,16]{1,0:T(8,128)S(1)}, f32[16,16]{1,0:T(8,128)S(1)}, s32[]{:T(128)}, s32[]{:T(128)}, /*index=5*/s32[]{:T(128)}) %tuple.1151), condition=%wide.region_32.33_spmd.clone.clone, body=%wide.region_29.32_spmd.clone.clone.sunk | while | flops 4755 | bytes 4584 | solution.py:74
  1320.1 23.5 %while.490 = (s32[]{:T(128)}, f32[16,16]{1,0:T(8,128)S(1)}, s32[]{:T(128)}) while((s32[]{:T(128)}, f32[16,16]{1,0:T(8,128)S(1)}, s32[]{:T(128)}) %tuple.1157), condition=%wide.region_41.42_spmd.clone.clone, body=%wide.region_37.41_spmd.clone.clone.sunk | while | flops 1905 | bytes 3897 | solution.py:104
  1348.8 25.0 %while.505 = (s32[]{:T(128)}, f32[16,16]{1,0:T(8,128)S(1)}, f32[16,16]{1,0:T(8,128)S(1)}, s32[]{:T(128)}, s32[]{:T(128)}, /*index=5*/s32[]{:T(128)}) while((s32[]{:T(128)}, f32[16,16]{1,0:T(8,128)S(1)}, f32[16,16]{1,0:T(8,128)S(1)}, s32[]{:T(128)}, s32[]{:T(128)}, /*index=5*/s32[]{:T(128)}) %tuple.1160), condition=%wide.region_45.46_spmd.clone.clone, body=%wide.region_42.45_spmd.clone.clone.sunk | while | flops 4755 | bytes 4584 | solution.py:74
  1378.6 23.5 %while.491 = (s32[]{:T(128)}, f32[16,16]{1,0:T(8,128)S(1)}, s32[]{:T(128)}) while((s32[]{:T(128)}, f32[16,16]{1,0:T(8,128)S(1)}, s32[]{:T(128)}) %tuple.1166), condition=%wide.region_53.54_spmd.clone.clone, body=%wide.region_49.53_spmd.clone.clone.sunk | while | flops 1905 | bytes 3897 | solution.py:104
  1407.3 25.0 %while.507 = (s32[]{:T(128)}, f32[16,16]{1,0:T(8,128)S(1)}, f32[16,16]{1,0:T(8,128)S(1)}, s32[]{:T(128)}, s32[]{:T(128)}, /*index=5*/s32[]{:T(128)}) while((s32[]{:T(128)}, f32[16,16]{1,0:T(8,128)S(1)}, f32[16,16]{1,0:T(8,128)S(1)}, s32[]{:T(128)}, s32[]{:T(128)}, /*index=5*/s32[]{:T(128)}) %tuple.1169), condition=%wide.region_57.58_spmd.clone.clone, body=%wide.region_54.57_spmd.clone.clone.sunk | while | flops 4755 | bytes 4584 | solution.py:74
  1437.0 23.5 %while.492 = (s32[]{:T(128)}, f32[16,16]{1,0:T(8,128)S(1)}, s32[]{:T(128)}) while((s32[]{:T(128)}, f32[16,16]{1,0:T(8,128)S(1)}, s32[]{:T(128)}) %tuple.1175), condition=%wide.region_65.66_spmd.clone.clone, body=%wide.region_61.65_spmd.clone.clone.sunk | while | flops 1905 | bytes 3897 | solution.py:104
  1465.7 25.0 %while.509 = (s32[]{:T(128)}, f32[16,16]{1,0:T(8,128)S(1)}, f32[16,16]{1,0:T(8,128)S(1)}, s32[]{:T(128)}, s32[]{:T(128)}, /*index=5*/s32[]{:T(128)}) while((s32[]{:T(128)}, f32[16,16]{1,0:T(8,128)S(1)}, f32[16,16]{1,0:T(8,128)S(1)}, s32[]{:T(128)}, s32[]{:T(128)}, /*index=5*/s32[]{:T(128)}) %tuple.1178), condition=%wide.region_69.70_spmd.clone.clone, body=%wide.region_66.69_spmd.clone.clone.sunk | while | flops 4755 | bytes 4584 | solution.py:74
  1495.1 23.5 %while.493 = (s32[]{:T(128)}, f32[16,16]{1,0:T(8,128)S(1)}, s32[]{:T(128)}) while((s32[]{:T(128)}, f32[16,16]{1,0:T(8,128)S(1)}, s32[]{:T(128)}) %tuple.1184), condition=%wide.region_77.78_spmd.clone.clone, body=%wide.region_73.77_spmd.clone.clone.sunk | while | flops 1905 | bytes 3897 | solution.py:104
  1523.8 25.0 %while.511 = (s32[]{:T(128)}, f32[16,16]{1,0:T(8,128)S(1)}, f32[16,16]{1,0:T(8,128)S(1)}, s32[]{:T(128)}, s32[]{:T(128)}, /*index=5*/s32[]{:T(128)}) while((s32[]{:T(128)}, f32[16,16]{1,0:T(8,128)S(1)}, f32[16,16]{1,0:T(8,128)S(1)}, s32[]{:T(128)}, s32[]{:T(128)}, /*index=5*/s32[]{:T(128)}) %tuple.1187), condition=%wide.region_81.82_spmd.clone.clone, body=%wide.region_78.81_spmd.clone.clone.sunk | while | flops 4755 | bytes 4584 | solution.py:74
  1582.0 25.0 %while.513 = (s32[]{:T(128)}, f32[16,16]{1,0:T(8,128)S(1)}, f32[16,16]{1,0:T(8,128)S(1)}, s32[]{:T(128)}, s32[]{:T(128)}, /*index=5*/s32[]{:T(128)}) while((s32[]{:T(128)}, f32[16,16]{1,0:T(8,128)S(1)}, f32[16,16]{1,0:T(8,128)S(1)}, s32[]{:T(128)}, s32[]{:T(128)}, /*index=5*/s32[]{:T(128)}) %tuple.1196), condition=%wide.region_93.94_spmd.clone.clone, body=%wide.region_90.93_spmd.clone.clone.sunk | while | flops 4755 | bytes 4584 | solution.py:74
  1640.8 25.0 %while.515 = (s32[]{:T(128)}, f32[16,16]{1,0:T(8,128)S(1)}, f32[16,16]{1,0:T(8,128)S(1)}, s32[]{:T(128)}, s32[]{:T(128)}, /*index=5*/s32[]{:T(128)}) while((s32[]{:T(128)}, f32[16,16]{1,0:T(8,128)S(1)}, f32[16,16]{1,0:T(8,128)S(1)}, s32[]{:T(128)}, s32[]{:T(128)}, /*index=5*/s32[]{:T(128)}) %tuple.1205), condition=%wide.region_105.106_spmd.clone.clone, body=%wide.region_102.105_spmd.clone.clone.sunk | while | flops 4755 | bytes 4584 | solution.py:74
  1668.6 23.5 %while.496 = (s32[]{:T(128)}, f32[16,16]{1,0:T(8,128)S(1)}, s32[]{:T(128)}) while((s32[]{:T(128)}, f32[16,16]{1,0:T(8,128)S(1)}, s32[]{:T(128)}) %tuple.1211), condition=%wide.region_113.114_spmd.clone.clone, body=%wide.region_109.113_spmd.clone.clone.sunk | while | flops 1905 | bytes 3897 | solution.py:104
  1693.6 111.2 %all-reduce.12.cloned.1.call-done = (f32[128,128]{0,1:T(8,128)}, f32[128,128]{0,1:T(8,128)}) async-done(((f32[128,128]{0,1:T(8,128)}, f32[128,128]{0,1:T(8,128)}), (f32[128,128]{0,1:T(8,128)}, f32[128,128]{0,1:T(8,128)})) %all-reduce.12.cloned.1.call-update) | async-done | bytes 131088 | tf_op jit(solution)/shard_map/psum | solution.py:21
  1805.8 211.7 %while.517 = (s32[]{:T(128)}, f32[128,128]{1,0:T(8,128)S(1)}, f32[128,128]{1,0:T(8,128)S(1)}, s32[]{:T(128)}, s32[]{:T(128)}, /*index=5*/s32[]{:T(128)}) while((s32[]{:T(128)}, f32[128,128]{1,0:T(8,128)S(1)}, f32[128,128]{1,0:T(8,128)S(1)}, s32[]{:T(128)}, s32[]{:T(128)}, /*index=5*/s32[]{:T(128)}) %tuple.1214), condition=%wide.region_119.120_spmd.clone.clone, body=%wide.region_116.119_spmd.clone.clone.sunk | while | flops 296067 | bytes 265208 | solution.py:74
  2018.5 52.0 %while.518 = (s32[]{:T(128)}, f32[128,128]{1,0:T(8,128)S(1)}, f32[128,128]{1,0:T(8,128)S(1)}, s32[]{:T(128)}, s32[]{:T(128)}) while((s32[]{:T(128)}, f32[128,128]{1,0:T(8,128)S(1)}, f32[128,128]{1,0:T(8,128)S(1)}, s32[]{:T(128)}, s32[]{:T(128)}) %tuple.1217), condition=%wide.region_123.124_spmd.clone.clone, body=%wide.region_121.123_spmd.clone.clone.sunk | while | flops 295555 | bytes 264664 | solution.py:88
  2074.5 93.3 %all-reduce.10.cloned.1.call-done = (f32[1024,128]{0,1:T(8,128)}, f32[128,128]{0,1:T(8,128)}) async-done(((f32[1024,128]{0,1:T(8,128)}, f32[128,128]{0,1:T(8,128)}), (f32[1024,128]{0,1:T(8,128)}, f32[128,128]{0,1:T(8,128)})) %all-reduce.10.cloned.1.call-update) | async-done | bytes 589840 | tf_op jit(solution)/shard_map/psum | solution.py:21
  2182.8 104.9 %all-reduce.8.cloned.1.call-done = f32[128,1536]{1,0:T(8,128)} async-done(((f32[128,1536]{1,0:T(8,128)}), f32[128,1536]{1,0:T(8,128)}) %all-reduce.8.cloned.1.call-update) | async-done | bytes 786448 | tf_op jit(solution)/shard_map/psum | solution.py:157
  (6828 shorter events, 1587.6 us)
Async XLA Ops:
  7.2 1797.7 %all-reduce.12.cloned.1.call-start = ((), (), s32[]{:S(2)}) async-start(), calls=%async_computation.2 | async-start | bytes 262144 | tf_op jit(solution)/shard_map/psum | solution.py:21
  208.4 3.2 collective-permute-start
  411.9 4.0 collective-permute-start.1
  630.7 4.7 collective-permute-start.2
  846.1 9.0 collective-permute-start.3
  1693.6 474.2 %all-reduce.10.cloned.1.call-start = ((), (), s32[]{:S(2)}) async-start(), calls=%async_computation.1 | async-start | bytes 1179648 | tf_op jit(solution)/shard_map/psum | solution.py:21
  2074.4 213.3 %all-reduce.8.cloned.1.call-start = ((), (), s32[]{:S(2)}) async-start(), calls=%async_computation | async-start | bytes 1572864 | tf_op jit(solution)/shard_map/psum | solution.py:157
  2175.2 6.9 copy-start.1
  2175.2 6.9 copy-start.2
  2175.2 114.5 %copy-start = (f32[1024,128]{0,1:T(8,128)S(1)}, f32[1024,128]{0,1:T(8,128)}, u32[]{:S(2)}) copy-start(f32[1024,128]{0,1:T(8,128)} %get-tuple-element.3669) | copy-start | bytes 1572868
Sparse Core Ops, SparseCore 0:
  1693.7 111.1 all-reduce.11
  2074.6 93.1 all-reduce.9
  2175.3 112.3 all-reduce.7
where the time goes:
time: 2330 us; the launch traced here: 2310 us
  other arithmetic  1080 us (46%)
  loops' own time  485 us (21%)
  matrix products  357 us (15%)
  waiting for transfers between devices  314 us (13%)
  local copies, waits for them, and re-layouts  46.8 us (2%)
    reduce_sum x1136, other arithmetic, pick_entry(): return jnp.sum(jnp.where(position == level, vector, 0.0))  714 us
    another operation x5, loops' own time, cholesky_upper(): remain, lower = lax.fori_loop(0, order, cholesky_advance, start)  469 us
    dot_general x634, matrix products, product(): return jnp.dot(left, right, precision=lax.Precision.HIGHEST)  345 us
    psum x2, waiting for transfers between devices, broadcast(): return lax.psum(kept, axis)  205 us
    psum x1, waiting for transfers between devices, per_device(): projected = lax.psum(inner_rows(reflectors, matrix), 'prow')  105 us
    select_n x128, other arithmetic, small_advance(): fixed_column = jnp.where(position > level, column, column_full)  83.2 us
    reduce_sum x768, other arithmetic, pick_column(): return jnp.sum(jnp.where((position == level)[None, :], square, 0.0), axis=1)  82.5 us
    reduce_sum x608, other arithmetic, pick_row(): return jnp.sum(jnp.where((position == level)[:, None], square, 0.0), axis=0)  58.8 us

commit v1 on v0

v1 whole, which is shorter than its diff:
```python
import functools
import jax
import jax.numpy as jnp
from jax import lax
from jax.experimental import pallas as pl
from jax.experimental.pallas import tpu as pltpu
from jax.sharding import PartitionSpec as P

B = 128
NB = 8
F32 = jnp.float32
BF16 = jnp.bfloat16
HI = lax.Precision.HIGHEST


def split3(x):
    h = x.astype(BF16).astype(F32)
    r = x - h
    m = r.astype(BF16).astype(F32)
    return h, m, r - m


def outer8(left, right):
    lh, lm, ll = split3(left)
    rh, rm, rl = split3(right)
    lhs = jnp.concatenate([lh, lh, lm, lm, lh, ll], axis=0).astype(BF16)
    rhs = jnp.concatenate([rh, rm, rh, rm, rl, rh], axis=0).astype(BF16)
    return lax.dot_general(lhs, rhs, (((0,), (0,)), ((), ())), preferred_element_type=F32)


def iotas():
    return (lax.broadcasted_iota(jnp.int32, (NB, B), 0), lax.broadcasted_iota(jnp.int32, (NB, B), 1))


def column(x, k0, i):
    return jnp.take_along_axis(x, jnp.full((NB, B), k0 + i, jnp.int32), axis=1, mode="promise_in_bounds")


def chol_block(k0, ga, r_out):
    row, lane = iotas()
    g = ga[pl.ds(k0, NB), :B]
    y = ga[pl.ds(k0, NB), B:]
    c = [column(g, k0, i) for i in range(NB)]
    ps = jnp.ones((NB, B), F32)
    pt = jnp.ones((NB, B), F32)
    cols = []
    for i in range(NB):
        p = jnp.broadcast_to(c[i][i:i + 1, :], (NB, B))
        m = jnp.where(row > i, c[i] * (1.0 / p), 0.0)
        ps = jnp.where(row == i, p, ps)
        cols.append((c[i], p))
        for a in range(i + 1, NB):
            c[a] = c[a] - m * c[a][i:i + 1, :]
        g, y = g - m * g[i:i + 1, :], y - m * y[i:i + 1, :]
    rs = root(ps)
    rb = jnp.where(lane >= k0 + row, g * rs, 0.0)
    yb = y * rs
    cr = [jnp.where(row <= i, c[i] * rs, 0.0) for i in range(NB)]
    rt = jnp.zeros((NB, B), F32)
    ct = []
    for i in range(NB):
        v = jnp.where(row >= i, cols[i][0] * jnp.broadcast_to(rs[i:i + 1, :], (NB, B)), 0.0)
        ct.append(v)
        rt = jnp.where(lane == k0 + i, v, rt)
    r_out[pl.ds(k0, NB), :] = rb
    ga[...] -= outer8(rb, jnp.concatenate([rb, yb], axis=1))
    return rb, yb, rt, tuple(cr), tuple(ct)


def root(x):
    r = lax.rsqrt(x)
    return r * (1.5 - 0.5 * x * r * r)


def lu_block(k0, rb, yb, rt, cr, crt, kb, kt, lt_out, u_out, z_out):
    row, lane = iotas()
    kr0 = kb[pl.ds(k0, NB), :B]
    kc0 = kt[pl.ds(k0, NB), :]
    b = kb[pl.ds(k0, NB), B:] + yb
    c = [column(kr0, k0, i) + cr[i] for i in range(NB)]
    ct = [column(kc0, k0, i) + crt[i] for i in range(NB)]
    kr, kc = kr0 + rb, kc0 + rt
    e = jnp.where(lane == k0 + row, 1.0, 0.0).astype(F32)
    ps = jnp.ones((NB, B), F32)
    for i in range(NB):
        p = jnp.broadcast_to(c[i][i:i + 1, :], (NB, B))
        inv = 1.0 / p
        m = jnp.where(row > i, c[i] * inv, 0.0)
        mt = jnp.where(row > i, ct[i] * inv, 0.0)
        ps = jnp.where(row == i, inv, ps)
        for a in range(i + 1, NB):
            c[a] = c[a] - m * c[a][i:i + 1, :]
            ct[a] = ct[a] - mt * ct[a][i:i + 1, :]
        kr, b = kr - m * kr[i:i + 1, :], b - m * b[i:i + 1, :]
        kc, e = kc - mt * kc[i:i + 1, :], e - mt * e[i:i + 1, :]
    ub = jnp.where(lane >= k0 + row, kr, 0.0)
    l = kc * ps
    e = e * ps
    inside = (lane >= k0) & (lane < k0 + NB)
    lp = jnp.where(inside, -e, l)
    lt_out[pl.ds(k0, NB), :] = jnp.where(lane > k0 + row, l, jnp.where(lane == k0 + row, 1.0, 0.0))
    u_out[pl.ds(k0, NB), :] = ub
    z_out[pl.ds(k0, NB), :] = b
    kb[pl.ds(k0, NB), :] = jnp.zeros((NB, 2 * B), F32)
    kb[...] -= outer8(lp, jnp.concatenate([ub, b], axis=1))
    lanes = lax.broadcasted_iota(jnp.int32, (B, B), 1)
    kt[...] = jnp.where((lanes >= k0) & (lanes < k0 + NB), 0.0, kt[...]) - outer8(ub, lp)


def eye():
    return jnp.where(lax.broadcasted_iota(jnp.int32, (B, B), 0) == lax.broadcasted_iota(jnp.int32, (B, B), 1), 1.0, 0.0).astype(F32)


def dot3(a, b, dims):
    return lax.dot_general(a, b, (dims, ((), ())), precision=HI, preferred_element_type=F32)


ROWS_L = 1024
COLS_L = 1536
PIECE = 96
NP = 16
NQ = 16
NZ = 8
CHUNK = ROWS_L // NQ
TURNS = COLS_L // B


def remote(src, dst, send_sem, recv_sem, **where):
    return pltpu.make_async_remote_copy(src_ref=src, dst_ref=dst, send_sem=send_sem, recv_sem=recv_sem,
                                        device_id=where, device_id_type=pl.DeviceIdType.MESH)


def each(count, body, start=0):
    def step(d, carry):
        body(d)
        return carry
    lax.fori_loop(start, count, step, 0)


def gather_kernel(a_hbm, p_out, wt_out, r_out, top_out, t_out, ui_out,
                  p_v, stage, at_h, at_l, a1t, a1b, ph2, ct, pair, cwb, ccwb, gl, gbuf, gp, wt,
                  ga, kb, kt, lt_s, u_s, z_s,
                  a_sem, p_sem, o_sem, ps_send, pp_send, p_recv, g_send, g_recv, h_send, h_recv,
                  gp_send, gp_recv, ga_send, ga_recv, a1_send, a1_recv, pr_send, pr_recv,
                  cw_send, cw_recv, ccw_send, ccw_recv, wc_send, wd_send, wp_send, w_recv):
    r = lax.axis_index("prow")
    q = lax.axis_index("pcol")
    z, core = lax.div(r, 2), lax.rem(r, 2)
    up = 2 * lax.rem(z + 1, NZ) + core
    down = 2 * lax.rem(z + NZ - 1, NZ) + core
    other = 2 * z + 1 - core
    first_col, first_row = q == 0, r == 0

    barrier = pltpu.get_barrier_semaphore()

    def greet_row(d):
        pl.semaphore_signal(barrier, inc=1, device_id={"prow": lax.rem(r + d, NP)}, device_id_type=pl.DeviceIdType.MESH)

    def greet_col(d):
        pl.semaphore_signal(barrier, inc=1, device_id={"pcol": lax.rem(q + d, NQ)}, device_id_type=pl.DeviceIdType.MESH)

    def load_panel():
        return pltpu.make_async_copy(a_hbm.at[:, pl.ds(0, B)], p_v, p_sem)

    def load(j):
        return pltpu.make_async_copy(a_hbm.at[:, pl.ds(pl.multiple_of(j * B, B), B)], stage.at[j], a_sem.at[j])

    @pl.when(first_col)
    def _():
        load_panel().start()

    each(NQ, greet_col, 1)
    each(NP, greet_row, 1)
    each(TURNS, lambda j: load(j).start())
    pl.semaphore_wait(barrier, NP + NQ - 2)

    def rows_of(ref, j, count):
        return ref.at[pl.ds(pl.multiple_of(j * count, count), count)]

    def scatter(j):
        return remote(rows_of(p_v, j, CHUNK), rows_of(p_v, j, CHUNK), ps_send.at[j], p_recv.at[j], pcol=j)

    def spread(mine, j):
        return remote(rows_of(p_v, mine, CHUNK), rows_of(p_v, mine, CHUNK), pp_send.at[j], p_recv.at[mine], pcol=j)

    def give_gram(j):
        return remote(rows_of(gl, j, NB), gbuf.at[r], g_send.at[j], g_recv.at[r], prow=j)

    def give_top(j):
        return remote(rows_of(p_v, j, NB), gp.at[j, pl.ds(NB, NB)], h_send.at[j], h_recv, prow=j)

    def plane(j):
        return remote(gp.at[r], gp.at[r], gp_send.at[j], gp_recv, pcol=j)

    def column_gather(d):
        j = lax.rem(r + d, NP)
        return remote(gp.at[r], gp.at[r], ga_send.at[j], ga_recv.at[r], prow=j)

    def turn(j):
        load(j).wait()
        block = stage[j].T
        h = block.astype(BF16)
        at = pl.ds(pl.multiple_of(j * B, B), B)
        at_h[at, :] = h
        at_l[at, :] = (block - h.astype(F32)).astype(BF16)
        a1t[at, :] = block[:, :B]

    @pl.when(first_col)
    def _():
        load_panel().wait()
        each(NQ, lambda j: scatter(j).start(), 1)
        each(NQ, lambda j: spread(0, j).start(), 1)
        gl[...] = dot3(p_v[...], p_v[...], ((0,), (0,)))
        each(NP, lambda d: give_gram(lax.rem(r + d, NP)).start(), 1)
        gbuf[pl.ds(r, 1)] = gl[pl.ds(pl.multiple_of(r * NB, NB), NB), :][None]

        @pl.when(first_row)
        def _():
            each(NP, lambda j: give_top(j).start(), 1)
            gp[0, NB:, :] = p_v[:NB, :]

    @pl.when(jnp.logical_not(first_col))
    def _():
        scatter(q).wait_recv()

        def pass_on(d):
            j = lax.rem(q + d, NQ)

            @pl.when(j != 0)
            def _():
                spread(q, j).start()

        each(NQ, pass_on, 1)

    each(TURNS // 2, turn)

    @pl.when(first_col)
    def _():
        def arrive(d):
            j = lax.rem(r + d, NP)
            remote(gbuf.at[j], gbuf.at[j], g_send.at[j], g_recv.at[j], prow=j).wait_recv()

        each(NP, arrive, 1)

        @pl.when(jnp.logical_not(first_row))
        def _():
            give_top(r).wait_recv()

        total = gbuf[0]
        for j in range(1, NP):
            total = total + gbuf[j]
        gp[pl.ds(r, 1), :NB, :] = total[None]
        each(NQ, lambda j: plane(j).start(), 1)

    @pl.when(jnp.logical_not(first_col))
    def _():
        plane(q).wait_recv()

    each(NP, lambda d: column_gather(d).start(), 1)
    each(TURNS, turn, TURNS // 2)

    def owner(j):
        return lax.rem(j, 2) * NZ + lax.div(j, 2)

    def give_a1(j):
        return remote(a1t.at[pl.ds(pl.multiple_of(owner(j) * PIECE, NB), PIECE)], a1b, a1_send.at[j], a1_recv, prow=j)

    @pl.when(first_row)
    def _():
        each(NP, lambda j: give_a1(j).start(), 1)
        a1b[...] = a1t[:PIECE, :]

    @pl.when(jnp.logical_not(first_col))
    def _():
        def arrive(d):
            j = lax.rem(q + d, NQ)
            remote(rows_of(p_v, j, CHUNK), rows_of(p_v, j, CHUNK), pp_send.at[j], p_recv.at[j], pcol=j).wait_recv()

        each(NQ, arrive, 1)

    keep_panel = pltpu.make_async_copy(p_v, p_out, o_sem.at[0])
    keep_panel.start()
    panel = p_v[...]
    ph = panel.astype(BF16)
    ph2[:, :B] = ph
    ph2[:, B:] = (panel - ph.astype(F32)).astype(BF16)

    def inner(start):
        def body(j):
            at = pl.ds(pl.multiple_of(start + j * B, B), B)
            both = jnp.dot(at_h[at, :], ph2[...], preferred_element_type=F32)
            low = jnp.dot(at_l[at, :], ph2[:, :B], preferred_element_type=F32)
            ct[at, :] = both[:, :B] + (both[:, B:] + low)
        return body

    half = NZ * PIECE
    theirs, ours = pl.multiple_of((1 - core) * half, half), pl.multiple_of(core * half, half)
    each(half // B, inner(theirs))
    swap = remote(ct.at[pl.ds(theirs, half)], pair, pr_send, pr_recv, prow=other)
    swap.start()
    each(half // B, inner(ours))

    def arrive_gram(d):
        j = lax.rem(r + d, NP)
        remote(gp.at[j], gp.at[j], ga_send.at[j], ga_recv.at[j], prow=j).wait_recv()

    each(NP, arrive_gram, 1)
    for j in range(NP):
        ga[NB * j:NB * (j + 1), :B] = gp[j, :NB, :]
        kb[NB * j:NB * (j + 1), :B] = gp[j, NB:, :]
    ga[:, B:] = eye()
    kb[:, B:] = jnp.zeros((B, B), F32)
    kt[...] = kb[:, :B].T

    def part(to):
        return pl.ds(pl.multiple_of(lax.rem(to + NZ, NZ) * PIECE, NB), PIECE)

    def send_up(s):
        return remote(pair.at[part(z + 5 - s)], cwb.at[s - 1], cw_send.at[s - 1], cw_recv.at[s - 1], prow=up)

    def send_down(s):
        return remote(pair.at[part(z - 4 + s)], ccwb.at[s - 1], ccw_send.at[s - 1], ccw_recv.at[s - 1], prow=down)

    def hop(s):
        if s == 0:
            swap.wait()
            pair[...] += ct[pl.ds(ours, half), :]
        else:
            send_up(s).wait_recv()
            pair[part(z + 4 - s), :] += cwb[s - 1]
            if s <= 3:
                send_down(s).wait_recv()
                pair[part(z - 3 + s), :] += ccwb[s - 1]
        if s < 4:
            send_up(s + 1).start()
        if s < 3:
            send_down(s + 1).start()

    state = chol_block(0, ga, r_out)

    def step(k, state):
        k0 = pl.multiple_of(k * NB, NB)
        lu_block(k0, *state, kb, kt, lt_s, u_s, z_s)
        return chol_block(pl.multiple_of(k0 + NB, NB), ga, r_out)

    for s in range(5):
        state = lax.fori_loop(3 * s, 3 * s + 3, step, state)
        hop(s)
    lu_block(B - NB, *state, kb, kt, lt_s, u_s, z_s)

    @pl.when(jnp.logical_not(first_row))
    def _():
        give_a1(r).wait_recv()

    m = kb[:, B:]
    total = pair[part(z), :] + dot3(a1b[...], r_out[...], ((1,), (0,)))
    mine = core * NZ + z
    wt[pl.ds(mine, 1)] = dot3(total, m, ((1,), (1,)))[None]

    def wsend(o, sem, to):
        return remote(wt.at[o], wt.at[o], sem, w_recv.at[o], prow=to)

    def wup(s):
        return wsend(core * NZ + lax.rem(z - s + NZ, NZ), wc_send.at[s], up)

    def wdown(s):
        return wsend(core * NZ + lax.rem(z + s, NZ), wd_send.at[s], down)

    def wacross(zz):
        return wsend(core * NZ + zz, wp_send.at[zz], other)

    wup(0).start()
    wdown(0).start()
    wacross(z).start()
    t_out[...] = dot3(u_s[...], z_s[...], ((1,), (1,)))
    ui_out[...] = dot3(m, dot3(r_out[...], lt_s[...], ((0,), (1,))), ((1,), (0,)))
    rows = lax.broadcasted_iota(jnp.int32, (B, B), 0)
    lanes = lax.broadcasted_iota(jnp.int32, (B, B), 1)
    top_out[...] = jnp.where(lanes >= rows, -r_out[...], lt_s[...].T)
    for s in range(1, 5):
        wup(s).wait_recv()
        if s < 4:
            wup(s).start()
        wacross(lax.rem(z - s + NZ, NZ)).start()
        if s < 4:
            wdown(s).wait_recv()
            if s < 3:
                wdown(s).start()
            wacross(lax.rem(z + s, NZ)).start()
    each(NZ, lambda zz: wsend((1 - core) * NZ + zz, wp_send.at[zz], other).wait_recv())
    keep = pltpu.make_async_copy(wt, wt_out, o_sem.at[1])
    keep.start()

    @pl.when(first_col)
    def _():
        each(NQ, lambda j: scatter(j).wait_send(), 1)
        each(NQ, lambda j: spread(0, j).wait_send(), 1)
        each(NP, lambda d: give_gram(lax.rem(r + d, NP)).wait_send(), 1)
        each(NQ, lambda j: plane(j).wait_send(), 1)

        @pl.when(first_row)
        def _():
            each(NP, lambda j: give_top(j).wait_send(), 1)

    @pl.when(jnp.logical_not(first_col))
    def _():
        def left(d):
            j = lax.rem(q + d, NQ)

            @pl.when(j != 0)
            def _():
                spread(q, j).wait_send()

        each(NQ, left, 1)

    @pl.when(first_row)
    def _():
        each(NP, lambda j: give_a1(j).wait_send(), 1)

    each(NP, lambda d: column_gather(d).wait_send(), 1)
    for s in range(4):
        send_up(s + 1).wait_send()
        wup(s).wait_send()
    for s in range(3):
        send_down(s + 1).wait_send()
        wdown(s).wait_send()
    each(NZ, lambda zz: wacross(zz).wait_send())
    keep_panel.wait()
    keep.wait()


def gather_call(matrix):
    sq = jax.ShapeDtypeStruct((B, B), F32)
    vm = pltpu.VMEM
    sem = pltpu.SemaphoreType.DMA
    anywhere = pl.BlockSpec(memory_space=pl.ANY)
    inside = pl.BlockSpec(memory_space=pltpu.VMEM)
    return pl.pallas_call(
        gather_kernel,
        out_shape=[jax.ShapeDtypeStruct((ROWS_L, B), F32), jax.ShapeDtypeStruct((NP, PIECE, B), F32)] + [sq] * 4,
        in_specs=[anywhere],
        out_specs=[anywhere, anywhere] + [inside] * 4,
        scratch_shapes=[
            vm((ROWS_L, B), F32), vm((TURNS, ROWS_L, B), F32), vm((COLS_L, ROWS_L), BF16), vm((COLS_L, ROWS_L), BF16),
            vm((COLS_L, B), F32), vm((PIECE, B), F32), vm((ROWS_L, 2 * B), BF16), vm((COLS_L, B), F32),
            vm((NZ * PIECE, B), F32), vm((4, PIECE, B), F32), vm((3, PIECE, B), F32), vm((B, B), F32),
            vm((NP, NB, B), F32), vm((NP, 2 * NB, B), F32), vm((NP, PIECE, B), F32),
            vm((B, 2 * B), F32), vm((B, 2 * B), F32), vm((B, B), F32), vm((B, B), F32), vm((B, B), F32), vm((B, B), F32),
            sem((TURNS,)), sem, sem((2,)), sem((NQ,)), sem((NQ,)), sem((NQ,)), sem((NP,)), sem((NP,)), sem((NP,)), sem,
            sem((NQ,)), sem, sem((NP,)), sem((NP,)), sem((NP,)), sem, sem, sem,
            sem((4,)), sem((4,)), sem((3,)), sem((3,)), sem((4,)), sem((3,)), sem((NZ,)), sem((NP,)),
        ],
        compiler_params=pltpu.CompilerParams(collective_id=0, has_side_effects=True, vmem_limit_bytes=40 * 2**20),
    )(matrix)


STRIP = 128


def update_kernel(flag, a_ref, p_ref, wt_ref, r_ref, top_ref, ui_ref, out_ref, w3):
    i = pl.program_id(0)

    @pl.when(i == 0)
    def _():
        w = wt_ref[...]
        h = w.astype(BF16)
        w3[:, :B] = h
        w3[:, B:2 * B] = (w - h.astype(F32)).astype(BF16)
        w3[:, 2 * B:] = h

    is_top = jnp.logical_and(flag[0] == 0, i == 0)
    plain = p_ref[...]
    p = plain + jnp.where(is_top, r_ref[...], 0.0)
    h = p.astype(BF16)
    left = jnp.concatenate([h, h, (p - h.astype(F32)).astype(BF16)], axis=1)
    gone = lax.dot_general(left, w3[...], (((1,), (1,)), ((), ())), preferred_element_type=F32)
    out_ref[...] = a_ref[...] - gone

    @pl.when(flag[1] == 0)
    def _():
        out_ref[:, :B] = jnp.where(is_top, top_ref[...], dot3(plain, ui_ref[...], ((1,), (0,))))


def update_call(flag, matrix, panel, wt, r, top, ui):
    whole = lambda shape: pl.BlockSpec(shape, lambda i: (0, 0))
    return pl.pallas_call(
        update_kernel,
        grid=(ROWS_L // STRIP,),
        out_shape=jax.ShapeDtypeStruct((ROWS_L, COLS_L), F32),
        in_specs=[pl.BlockSpec(memory_space=pltpu.SMEM), pl.BlockSpec((STRIP, COLS_L), lambda i: (i, 0)),
                  pl.BlockSpec((STRIP, B), lambda i: (i, 0)), whole((COLS_L, B)), whole((B, B)), whole((B, B)), whole((B, B))],
        out_specs=pl.BlockSpec((STRIP, COLS_L), lambda i: (i, 0)),
        scratch_shapes=[pltpu.VMEM((COLS_L, 3 * B), BF16)],
        compiler_params=pltpu.CompilerParams(vmem_limit_bytes=24 * 2**20),
    )(flag, matrix, panel, wt, r, top, ui)


def per_device(matrix):
    flag = jnp.stack([lax.axis_index("prow"), lax.axis_index("pcol")]).astype(jnp.int32)
    panel, wt, r, top, t, ui = gather_call(matrix)
    factored = update_call(flag, matrix, panel, wt.reshape(COLS_L, B), r, top, ui)
    return factored, t


def solution(mesh):
    return jax.shard_map(
        per_device,
        mesh=mesh,
        in_specs=(P("prow", "pcol"),),
        out_specs=(P("prow", "pcol"), P()),
        check_vma=False,
    )
```

time: 2330 us -> 74.4 us (0.03)
  other arithmetic: 1080 us -> 0.08 us
  loops' own time: 485 us -> 0 us
  matrix products: 357 us -> 0 us
  waiting for transfers between devices: 314 us -> 0 us
  Pallas kernels: 0 us -> 69.5 us
  local copies, waits for them, and re-layouts: 46.8 us -> 3.41 us
    reduce_sum x2512 -> x0, other arithmetic: 855 us -> none  [the longest x1136 714 us: pick_entry(): return jnp.sum(jnp.where(position == level, vector, 0.0))]
    another operation x30 -> x0, loops' own time: 485 us -> none  [the longest x5 469 us: cholesky_upper(): remain, lower = lax.fori_loop(0, order, cholesky_advance, start)]
    dot_general x644 -> x0, matrix products: 357 us -> none  [the longest x634 345 us: product(): return jnp.dot(left, right, precision=lax.Precision.HIGHEST)]
    psum x3 -> x0, waiting for transfers between devices: 309 us -> none  [the longest x2 205 us: broadcast(): return lax.psum(kept, axis)]
    add x1260 -> x0, other arithmetic: 117 us -> none  [the longest x640 57.5 us: cholesky_advance(): lower + jnp.where((position == level)[None, :], column[:, None], 0.0)]
    select_n x898 -> x0, other arithmetic: 97.4 us -> none  [the longest x128 83.2 us: small_advance(): fixed_column = jnp.where(position > level, column, column_full)]
    pallas_call x0 -> x2, Pallas kernels: none -> 69.5 us  [the longest x1 62.5 us: gather_call(): pl.pallas_call(gather_kernel, out_shape=[jax.ShapeDtypeStruct((ROWS_L, B)...]
    scatter x29 -> x0, local copies, waits for them, and re-layouts: 26.4 us -> none  [the longest x7 7.83 us: split_triangles(): packed = packed.at[start:finish, finish:].set(row_part)]
where the time goes in v1:
time: 74.4 us; the launch traced here: 73.6 us
  Pallas kernels  69.5 us (93%)
  local copies, waits for them, and re-layouts  3.41 us (5%)
    pallas_call x1, Pallas kernels, gather_call(): pl.pallas_call(gather_kernel, out_shape=[jax.ShapeDtypeStruct((ROWS_L, B)...  62.5 us
    pallas_call x1, Pallas kernels, update_call(): pl.pallas_call(update_kernel, grid=(ROWS_L // STRIP,), out_shape=jax.Shap...  6.94 us
    unnamed x3, local copies, waits for them, and re-layouts  3.41 us

profile of v1, /device:TPU:25, one launch (start us, length us, event | category | flops | bytes accessed | tf_op | source)
XLA Modules:
  0.0 73.6 jit_solution(3207742043547558676)
XLA Ops:
  0.6 0.1 pad_add_fusion.flag
  0.7 0.0 copy-start
  0.7 2.8 %copy-done = f32[1024,1536]{1,0:T(8,128)S(1)} copy-done((f32[1024,1536]{1,0:T(8,128)S(1)}, f32[1024,1536]{1,0:T(8,128)}, u32[]{:S(2)}) %copy-start) | copy-done | bytes 6291480
  3.5 62.5 %shard_map.30 = (f32[1024,128]{1,0:T(8,128)S(1)}, f32[16,96,128]{2,1,0:T(8,128)S(1)}, f32[128,128]{1,0:T(8,128)S(1)}, f32[128,128]{1,0:T(8,128)S(1)}, f32[128,128]{1,0:T(8,128)S(1)}, /*index=5*/f32[128,128]{1,0:T(8,128)S(1)}) custom-call(f32[1024,1536]{1,0:T(8,128)S(1)} %copy-done), custom_call_target="tpu_custom_call" | custom-call | tf_op jit(solution)/shard_map/pallas_call | solution.py:438
  66.0 6.9 %shard_map.31 = f32[1024,1536]{1,0:T(8,128)} custom-call(s32[2]{0:T(128)S(1)} %pad_add_fusion.flag, f32[1024,1536]{1,0:T(8,128)S(1)} %copy-done, f32[1024,128]{1,0:T(8,128)S(1)} %get-tuple-element.8.p_ref, f32[1536,128]{1,0:T(8,128)S(1)} %bitcast.3, f32[128,128]{1,0:T(8,128)S(1)} %get-tuple-element.10.r_ref, f32[128,128]{1,0:T(8,128)S(1)} %get-tuple-element.11.top_ref, ...), custom_call_target="tpu_custom_call" | custom-call | tf_op jit(solution)/shard_map/pallas_call | solution.py:486
  73.0 0.6 copy.4
Async XLA Ops:
  0.7 2.8 %copy-start = (f32[1024,1536]{1,0:T(8,128)S(1)}, f32[1024,1536]{1,0:T(8,128)}, u32[]{:S(2)}) copy-start(f32[1024,1536]{1,0:T(8,128)} %a_ref.1) | copy-start | bytes 18874372

commit v2 on v1

v2 whole, which is shorter than its diff:
```python
import functools
import jax
import jax.numpy as jnp
from jax import lax
from jax.experimental import pallas as pl
from jax.experimental.pallas import tpu as pltpu
from jax.sharding import PartitionSpec as P

B = 128
NB = 8
F32 = jnp.float32
BF16 = jnp.bfloat16
HI = lax.Precision.HIGHEST


def split3(x):
    h = x.astype(BF16).astype(F32)
    r = x - h
    m = r.astype(BF16).astype(F32)
    return h, m, r - m


def outer8(left, right):
    lh, lm, ll = split3(left)
    rh, rm, rl = split3(right)
    lhs = jnp.concatenate([lh, lh, lm, lm, lh, ll], axis=0).astype(BF16)
    rhs = jnp.concatenate([rh, rm, rh, rm, rl, rh], axis=0).astype(BF16)
    return lax.dot_general(lhs, rhs, (((0,), (0,)), ((), ())), preferred_element_type=F32)


def iotas():
    return (lax.broadcasted_iota(jnp.int32, (NB, B), 0), lax.broadcasted_iota(jnp.int32, (NB, B), 1))


def column(x, k0, i):
    return jnp.take_along_axis(x, jnp.full((NB, B), k0 + i, jnp.int32), axis=1, mode="promise_in_bounds")


def chol_block(k0, ga, r_out):
    row, lane = iotas()
    g = ga[pl.ds(k0, NB), :B]
    y = ga[pl.ds(k0, NB), B:]
    c = [column(g, k0, i) for i in range(NB)]
    ps = jnp.ones((NB, B), F32)
    pt = jnp.ones((NB, B), F32)
    cols = []
    for i in range(NB):
        p = jnp.broadcast_to(c[i][i:i + 1, :], (NB, B))
        m = jnp.where(row > i, c[i] * (1.0 / p), 0.0)
        ps = jnp.where(row == i, p, ps)
        cols.append((c[i], p))
        for a in range(i + 1, NB):
            c[a] = c[a] - m * c[a][i:i + 1, :]
        g, y = g - m * g[i:i + 1, :], y - m * y[i:i + 1, :]
    rs = root(ps)
    rb = jnp.where(lane >= k0 + row, g * rs, 0.0)
    yb = y * rs
    cr = [jnp.where(row <= i, c[i] * rs, 0.0) for i in range(NB)]
    rt = jnp.zeros((NB, B), F32)
    ct = []
    for i in range(NB):
        v = jnp.where(row >= i, cols[i][0] * jnp.broadcast_to(rs[i:i + 1, :], (NB, B)), 0.0)
        ct.append(v)
        rt = jnp.where(lane == k0 + i, v, rt)
    r_out[pl.ds(k0, NB), :] = rb
    ga[...] -= outer8(rb, jnp.concatenate([rb, yb], axis=1))
    return rb, yb, rt, tuple(cr), tuple(ct)


def root(x):
    r = lax.rsqrt(x)
    return r * (1.5 - 0.5 * x * r * r)


def lu_block(k0, rb, yb, rt, cr, crt, kb, kt, lt_out, u_out, z_out):
    row, lane = iotas()
    kr0 = kb[pl.ds(k0, NB), :B]
    kc0 = kt[pl.ds(k0, NB), :]
    b = kb[pl.ds(k0, NB), B:] + yb
    c = [column(kr0, k0, i) + cr[i] for i in range(NB)]
    ct = [column(kc0, k0, i) + crt[i] for i in range(NB)]
    kr, kc = kr0 + rb, kc0 + rt
    e = jnp.where(lane == k0 + row, 1.0, 0.0).astype(F32)
    ps = jnp.ones((NB, B), F32)
    for i in range(NB):
        p = jnp.broadcast_to(c[i][i:i + 1, :], (NB, B))
        inv = 1.0 / p
        m = jnp.where(row > i, c[i] * inv, 0.0)
        mt = jnp.where(row > i, ct[i] * inv, 0.0)
        ps = jnp.where(row == i, inv, ps)
        for a in range(i + 1, NB):
            c[a] = c[a] - m * c[a][i:i + 1, :]
            ct[a] = ct[a] - mt * ct[a][i:i + 1, :]
        kr, b = kr - m * kr[i:i + 1, :], b - m * b[i:i + 1, :]
        kc, e = kc - mt * kc[i:i + 1, :], e - mt * e[i:i + 1, :]
    ub = jnp.where(lane >= k0 + row, kr, 0.0)
    l = kc * ps
    e = e * ps
    inside = (lane >= k0) & (lane < k0 + NB)
    lp = jnp.where(inside, -e, l)
    lt_out[pl.ds(k0, NB), :] = jnp.where(lane > k0 + row, l, jnp.where(lane == k0 + row, 1.0, 0.0))
    u_out[pl.ds(k0, NB), :] = ub
    z_out[pl.ds(k0, NB), :] = b
    kb[pl.ds(k0, NB), :] = jnp.zeros((NB, 2 * B), F32)
    kb[...] -= outer8(lp, jnp.concatenate([ub, b], axis=1))
    lanes = lax.broadcasted_iota(jnp.int32, (B, B), 1)
    kt[...] = jnp.where((lanes >= k0) & (lanes < k0 + NB), 0.0, kt[...]) - outer8(ub, lp)


def eye():
    return jnp.where(lax.broadcasted_iota(jnp.int32, (B, B), 0) == lax.broadcasted_iota(jnp.int32, (B, B), 1), 1.0, 0.0).astype(F32)


def dot3(a, b, dims):
    return lax.dot_general(a, b, (dims, ((), ())), precision=HI, preferred_element_type=F32)


ROWS_L = 1024
COLS_L = 1536
PIECE = 96
NP = 16
NQ = 16
NZ = 8
CHUNK = ROWS_L // NQ
TURNS = COLS_L // B


def remote(src, dst, send_sem, recv_sem, **where):
    return pltpu.make_async_remote_copy(src_ref=src, dst_ref=dst, send_sem=send_sem, recv_sem=recv_sem,
                                        device_id=where, device_id_type=pl.DeviceIdType.MESH)


def each(count, body, start=0):
    def step(d, carry):
        body(d)
        return carry
    lax.fori_loop(start, count, step, 0)


GROUPS = 4
GROUP = ROWS_L // GROUPS
FAR = (4, 3, 5, 2, 6, 1, 7)
NEAR = (1, 7, 2, 6, 3, 5, 4)


def factor_kernel(a_hbm, out, t_out,
                  p_v, a_v, at_h, at_l, a1t, a1b, ph2, ct, pair, rsb, gl, gbuf, gp, wt, pk, v2,
                  ga, kb, kt, r_s, lt_s, u_s, z_s,
                  a_sem, p_sem, ps_send, pp_send, p_recv, g_send, g_recv, h_send, h_recv,
                  gp_send, gp_recv, ga_send, ga_recv, a1_send, a1_recv, pr_send, pr_recv,
                  rs_send, rs_recv, wd_send, wp_send, w_recv):
    r = lax.axis_index("prow")
    q = lax.axis_index("pcol")
    z, core = lax.div(r, 2), lax.rem(r, 2)
    other = 2 * z + 1 - core
    first_col, first_row = q == 0, r == 0

    barrier = pltpu.get_barrier_semaphore()

    def greet_row(d):
        pl.semaphore_signal(barrier, inc=1, device_id={"prow": lax.rem(r + d, NP)}, device_id_type=pl.DeviceIdType.MESH)

    def greet_col(d):
        pl.semaphore_signal(barrier, inc=1, device_id={"pcol": lax.rem(q + d, NQ)}, device_id_type=pl.DeviceIdType.MESH)

    def load_panel():
        return pltpu.make_async_copy(a_hbm.at[:, pl.ds(0, B)], p_v, p_sem)

    def load(j):
        at = pl.ds(pl.multiple_of(j * B, B), B)
        return pltpu.make_async_copy(a_hbm.at[:, at], a_v.at[:, at], a_sem.at[j])

    @pl.when(first_col)
    def _():
        load_panel().start()

    each(NQ, greet_col, 1)
    each(NP, greet_row, 1)
    each(TURNS, lambda j: load(j).start())
    pl.semaphore_wait(barrier, NP + NQ - 2)

    def rows_of(ref, j, count):
        return ref.at[pl.ds(pl.multiple_of(j * count, count), count)]

    def scatter(j):
        return remote(rows_of(p_v, j, CHUNK), rows_of(p_v, j, CHUNK), ps_send.at[j], p_recv.at[j], pcol=j)

    def spread_in(j):
        return remote(rows_of(p_v, j, CHUNK), rows_of(p_v, j, CHUNK), pp_send.at[j], p_recv.at[j], pcol=j)

    def spread(mine, j):
        return remote(rows_of(p_v, mine, CHUNK), rows_of(p_v, mine, CHUNK), pp_send.at[j], p_recv.at[mine], pcol=j)

    def give_gram(j):
        return remote(rows_of(gl, j, NB), gbuf.at[r], g_send.at[j], g_recv.at[r], prow=j)

    def give_top(j):
        return remote(rows_of(p_v, j, NB), gp.at[j, pl.ds(NB, NB)], h_send.at[j], h_recv, prow=j)

    def plane(j):
        return remote(gp.at[r], gp.at[r], gp_send.at[j], gp_recv, pcol=j)

    def column_gather(d):
        j = lax.rem(r + d, NP)
        return remote(gp.at[r], gp.at[r], ga_send.at[j], ga_recv.at[r], prow=j)

    def turn(j):
        load(j).wait()
        at = pl.ds(pl.multiple_of(j * B, B), B)
        block = a_v[:, at].T
        h = block.astype(BF16)
        at_h[at, :] = h
        at_l[at, :] = (block - h.astype(F32)).astype(BF16)
        a1t[at, :] = block[:, :B]

    @pl.when(first_col)
    def _():
        load_panel().wait()
        each(NQ, lambda j: scatter(j).start(), 1)
        each(NQ, lambda j: spread(0, j).start(), 1)
        gl[...] = dot3(p_v[...], p_v[...], ((0,), (0,)))
        each(NP, lambda d: give_gram(lax.rem(r + d, NP)).start(), 1)
        gbuf[pl.ds(r, 1)] = gl[pl.ds(pl.multiple_of(r * NB, NB), NB), :][None]

        @pl.when(first_row)
        def _():
            each(NP, lambda j: give_top(j).start(), 1)
            gp[0, NB:, :] = p_v[:NB, :]

    @pl.when(jnp.logical_not(first_col))
    def _():
        scatter(q).wait_recv()

        def pass_on(d):
            j = lax.rem(q + d, NQ)

            @pl.when(j != 0)
            def _():
                spread(q, j).start()

        each(NQ, pass_on, 1)

    each(TURNS // 2, turn)

    @pl.when(first_col)
    def _():
        def arrive(d):
            j = lax.rem(r + d, NP)
            remote(gbuf.at[j], gbuf.at[j], g_send.at[j], g_recv.at[j], prow=j).wait_recv()

        each(NP, arrive, 1)

        @pl.when(jnp.logical_not(first_row))
        def _():
            give_top(r).wait_recv()

        total = gbuf[0]
        for j in range(1, NP):
            total = total + gbuf[j]
        gp[pl.ds(r, 1), :NB, :] = total[None]
        each(NQ, lambda j: plane(j).start(), 1)
        each(NP, lambda d: column_gather(d).start(), 1)

    def give_a1(j):
        return remote(a1t.at[pl.ds(pl.multiple_of(j * PIECE, NB), PIECE)], a1b, a1_send.at[j], a1_recv, prow=j)

    each(TURNS, turn, TURNS // 2)

    @pl.when(first_row)
    def _():
        each(NP, lambda j: give_a1(j).start(), 1)
        a1b[...] = a1t[:PIECE, :]

    def group(step):
        return lax.rem(lax.div(q, GROUPS) + (0, 1, 3, 2)[step], GROUPS)

    def arrive_group(step):
        @pl.when(jnp.logical_not(first_col))
        def _():
            def arrive(d):
                j = group(step) * GROUPS + d

                @pl.when(j != q)
                def _():
                    spread_in(j).wait_recv()

            each(GROUPS, arrive)

        at = pl.ds(pl.multiple_of(group(step) * GROUP, GROUP), GROUP)
        panel = p_v[at, :]
        ph = panel.astype(BF16)
        ph2[:, :B] = ph
        ph2[:, B:] = (panel - ph.astype(F32)).astype(BF16)

    def inner(step):
        arrive_group(step)
        along = pl.ds(pl.multiple_of(group(step) * GROUP, GROUP), GROUP)
        both = jnp.dot(at_h[:, along], ph2[...], preferred_element_type=F32)
        low = jnp.dot(at_l[:, along], ph2[:, :B], preferred_element_type=F32)
        sums = both[:, :B] + (both[:, B:] + low)
        if step == 0:
            ct[...] = sums
        else:
            ct[...] += sums

    @pl.when(jnp.logical_not(first_col))
    def _():
        plane(q).wait_recv()
        each(NP, lambda d: column_gather(d).start(), 1)

    for step in range(GROUPS):
        inner(step)

    def ring(d):
        return lax.rem(z + d, NZ)

    def swap(to):
        theirs = pl.ds(pl.multiple_of((2 * to + 1 - core) * PIECE, 32), PIECE)
        return remote(ct.at[theirs], pair.at[to], pr_send.at[to], pr_recv.at[to], prow=other)

    def reduce_to(to):
        return remote(pair.at[to], rsb.at[z], rs_send.at[to], rs_recv.at[z], prow=2 * to + core)

    def far(d):
        return ring(jnp.where(d == NZ - 1, NZ, NZ // 2 + jnp.where(lax.rem(d, 2) == 0, 1, -1) * lax.div(d + 1, 2)))

    def ours_step(d):
        to = far(d)
        swap(to).wait_recv()
        pair[pl.ds(to, 1)] += ct[pl.ds(pl.multiple_of((2 * to + core) * PIECE, 32), PIECE), :][None]

        @pl.when(to != z)
        def _():
            reduce_to(to).start()

    each(NZ, lambda d: swap(far(d)).start())
    each(NZ, ours_step)

    def arrive_gram(d):
        j = lax.rem(r + d, NP)
        remote(gp.at[j], gp.at[j], ga_send.at[j], ga_recv.at[j], prow=j).wait_recv()

    each(NP, arrive_gram, 1)
    for j in range(NP):
        ga[NB * j:NB * (j + 1), :B] = gp[j, :NB, :]
        kb[NB * j:NB * (j + 1), :B] = gp[j, NB:, :]
    ga[:, B:] = eye()
    kb[:, B:] = jnp.zeros((B, B), F32)
    kt[...] = kb[:, :B].T

    state = chol_block(0, ga, r_s)

    def step(k, state):
        k0 = pl.multiple_of(k * NB, NB)
        lu_block(k0, *state, kb, kt, lt_s, u_s, z_s)
        return chol_block(pl.multiple_of(k0 + NB, NB), ga, r_s)

    state = lax.fori_loop(0, B // NB - 1, step, state)
    lu_block(B - NB, *state, kb, kt, lt_s, u_s, z_s)

    @pl.when(jnp.logical_not(first_row))
    def _():
        give_a1(r).wait_recv()

    m = kb[:, B:]
    total = pair[pl.ds(z, 1)][0] + dot3(a1b[...], r_s[...], ((1,), (0,)))
    for d in FAR:
        remote(rsb.at[ring(d)], rsb.at[ring(d)], rs_send.at[ring(d)], rs_recv.at[ring(d)], prow=r).wait_recv()
    for d in FAR:
        total = total + rsb[pl.ds(ring(d), 1)][0]
    wt[pl.ds(r, 1)] = dot3(total, m, ((1,), (1,)))[None]

    def wsend(o, sem, to):
        return remote(wt.at[o], wt.at[o], sem, w_recv.at[o], prow=to)

    def wout(d):
        return wsend(r, wd_send.at[d], 2 * ring(d) + core)

    def wacross(zz):
        return wsend(2 * zz + core, wp_send.at[zz], other)

    wacross(z).start()
    for d in (2, 6, 1, 7, 4, 3, 5):
        wout(d).start()

    t_out[...] = dot3(u_s[...], z_s[...], ((1,), (1,)))
    plain = p_v[...]
    p = jnp.concatenate([plain[:B] + jnp.where(first_row, r_s[...], 0.0), plain[B:]], axis=0)
    h = p.astype(BF16)
    pk[:, :B] = h
    pk[:, B:2 * B] = h
    pk[:, 2 * B:] = (p - h.astype(F32)).astype(BF16)

    @pl.when(first_col)
    def _():
        v2[...] = dot3(p_v[...], dot3(m, dot3(r_s[...], lt_s[...], ((0,), (1,))), ((1,), (0,))), ((1,), (0,)))

        @pl.when(first_row)
        def _():
            rows = lax.broadcasted_iota(jnp.int32, (B, B), 0)
            lanes = lax.broadcasted_iota(jnp.int32, (B, B), 1)
            v2[:B, :] = jnp.where(lanes >= rows, -r_s[...], lt_s[...].T)

    def come(o):
        wsend(o, wp_send.at[0], other).wait_recv()

    def come_and_pass(d):
        come(2 * ring(d) + core)
        wacross(ring(d)).start()

    def update(g):
        for zz in (2 * g, 2 * g + 1):
            come(2 * zz + 1 - core)
        w = wt[pl.ds(4 * g, 4)].reshape(4 * PIECE, B)
        wh = w.astype(BF16)
        w3 = jnp.concatenate([wh, (w - wh.astype(F32)).astype(BF16), wh], axis=1)
        cols = pl.ds(pl.multiple_of(g * 4 * PIECE, B), 4 * PIECE)

        out[:, cols] = a_v[:, cols] - lax.dot_general(
            pk[...], w3, (((1,), (1,)), ((), ())), preferred_element_type=F32)

    half, odd = lax.div(z, 2), lax.rem(z, 2)
    inner_group = lax.rem(half + 3 + 2 * odd, GROUPS)
    outer_group = lax.rem(half + 1 + 2 * odd, GROUPS)
    for d in (1, 7, 2, 6):
        come_and_pass(d)
    update(half)
    update(inner_group)
    for d in (3, 5):
        come_and_pass(d)
    update(outer_group)
    come_and_pass(4)
    update(lax.rem(half + 2, GROUPS))

    @pl.when(first_col)
    def _():
        out[:, :B] = v2[...]

    @pl.when(first_col)
    def _():
        each(NQ, lambda j: scatter(j).wait_send(), 1)
        each(NQ, lambda j: spread(0, j).wait_send(), 1)
        each(NP, lambda d: give_gram(lax.rem(r + d, NP)).wait_send(), 1)
        each(NQ, lambda j: plane(j).wait_send(), 1)

        @pl.when(first_row)
        def _():
            each(NP, lambda j: give_top(j).wait_send(), 1)

    @pl.when(jnp.logical_not(first_col))
    def _():
        def left(d):
            j = lax.rem(q + d, NQ)

            @pl.when(j != 0)
            def _():
                spread(q, j).wait_send()

        each(NQ, left, 1)

    @pl.when(first_row)
    def _():
        each(NP, lambda j: give_a1(j).wait_send(), 1)

    each(NP, lambda d: column_gather(d).wait_send(), 1)
    each(NZ, lambda to: swap(to).wait_send())
    for d in FAR:
        reduce_to(ring(d)).wait_send()
        wout(d).wait_send()
    each(NZ, lambda zz: wacross(zz).wait_send())


def factor_call(matrix):
    vm = pltpu.VMEM
    sem = pltpu.SemaphoreType.DMA
    square = vm((B, B), F32)
    return pl.pallas_call(
        factor_kernel,
        out_shape=[vm((ROWS_L, COLS_L), F32), vm((B, B), F32)],
        in_specs=[pl.BlockSpec(memory_space=pltpu.HBM)],
        out_specs=[pl.BlockSpec(memory_space=pltpu.VMEM)] * 2,
        scratch_shapes=[
            vm((ROWS_L, B), F32), vm((ROWS_L, COLS_L), F32), vm((COLS_L, ROWS_L), BF16), vm((COLS_L, ROWS_L), BF16),
            vm((COLS_L, B), F32), vm((PIECE, B), F32), vm((GROUP, 2 * B), BF16), vm((COLS_L, B), F32),
            vm((NZ, PIECE, B), F32), vm((NZ, PIECE, B), F32), square,
            vm((NP, NB, B), F32), vm((NP, 2 * NB, B), F32), vm((NP, PIECE, B), F32), vm((ROWS_L, 3 * B), BF16),
            vm((ROWS_L, B), F32),
            vm((B, 2 * B), F32), vm((B, 2 * B), F32), square, square, square, square, square,
            sem((TURNS,)), sem, sem((NQ,)), sem((NQ,)), sem((NQ,)), sem((NP,)), sem((NP,)),
            sem((NP,)), sem, sem((NQ,)), sem, sem((NP,)), sem((NP,)), sem((NP,)), sem, sem((NZ,)), sem((NZ,)),
            sem((NZ,)), sem((NZ,)), sem((NZ,)), sem((NZ,)), sem((NP,)),
        ],
        compiler_params=pltpu.CompilerParams(collective_id=0, has_side_effects=True, vmem_limit_bytes=40 * 2**20),
    )(pltpu.with_memory_space_constraint(matrix, pltpu.HBM))


PARTS = 8


def store_kernel(x, t, out, t_out, sem):
    copies = [pltpu.make_async_copy(t, t_out, sem.at[PARTS])]
    for i in range(PARTS):
        at = pl.ds(i * (ROWS_L // PARTS), ROWS_L // PARTS)
        copies.append(pltpu.make_async_copy(x.at[at], out.at[at], sem.at[i]))
    for copy in copies:
        copy.start()
    for copy in copies:
        copy.wait()


def store_call(x, t):
    return pl.pallas_call(
        store_kernel,
        out_shape=[pltpu.HBM(x.shape, F32), pltpu.HBM(t.shape, F32)],
        in_specs=[pl.BlockSpec(memory_space=pltpu.VMEM)] * 2,
        out_specs=[pl.BlockSpec(memory_space=pltpu.HBM)] * 2,
        scratch_shapes=[pltpu.SemaphoreType.DMA((PARTS + 1,))],
        compiler_params=pltpu.CompilerParams(vmem_limit_bytes=16 * 2**20),
    )(pltpu.with_memory_space_constraint(x, pltpu.VMEM), pltpu.with_memory_space_constraint(t, pltpu.VMEM))


def per_device(matrix):
    return tuple(store_call(*factor_call(matrix)))


def solution(mesh):
    return jax.shard_map(
        per_device,
        mesh=mesh,
        in_specs=(P("prow", "pcol"),),
        out_specs=(P("prow", "pcol"), P()),
        check_vma=False,
    )
```

time: 74.4 us -> 59.9 us (0.81)
  the two profiles are of different devices: /device:TPU:25 before, /device:TPU:61 now
where the time goes in v2:
time: 59.9 us; the launch traced here: 59.8 us
  Pallas kernels  59.1 us (99%)
  between operations  0.64 us (1%)
    pallas_call x1, Pallas kernels, factor_call(): pl.pallas_call(factor_kernel, out_shape=[vm((ROWS_L, COLS_L), F32), vm((B...  56.4 us
    pallas_call x1, Pallas kernels, store_call(): pl.pallas_call(store_kernel, out_shape=[pltpu.HBM(x.shape, F32), pltpu.HB...  2.77 us

profile of v2, /device:TPU:61, one launch (start us, length us, event | category | flops | bytes accessed | tf_op | source)
XLA Modules:
  0.0 59.8 jit_solution(10489738637557428841)
XLA Ops:
  0.6 56.4 %shard_map.30 = (f32[1024,1536]{1,0:T(8,128)S(1)}, f32[128,128]{1,0:T(8,128)S(1)}) custom-call(f32[1024,1536]{1,0:T(8,128)} %a_hbm.1), custom_call_target="tpu_custom_call" | custom-call | tf_op jit(solution)/shard_map/pallas_call | solution.py:477
  57.0 2.8 %shard_map.31 = (f32[1024,1536]{1,0:T(8,128)}, f32[128,128]{1,0:T(8,128)}) custom-call(f32[1024,1536]{1,0:T(8,128)S(1)} %get-tuple-element.4.x, f32[128,128]{1,0:T(8,128)S(1)} %get-tuple-element.5.t), custom_call_target="tpu_custom_call" | custom-call | tf_op jit(solution)/shard_map/pallas_call | solution.py:512

commit v3 on v2

--- a/solution.py
+++ b/solution.py
@@ -140,7 +140,9 @@
 GROUPS = 4
 GROUP = ROWS_L // GROUPS
 FAR = (4, 3, 5, 2, 6, 1, 7)
-NEAR = (1, 7, 2, 6, 3, 5, 4)
+SENT = (2, 6, 1, 7)
+FAR_ROWS = (8, 9, 7, 10, 6, 11, 5, 12, 4, 13, 3, 14, 2, 15, 1)
+FAR_COLS = (10, 9, 11, 8, 6, 14, 5, 7, 13, 15, 4, 12, 2, 1, 3)
 
 
 def factor_kernel(a_hbm, out, t_out,
@@ -148,7 +150,7 @@
                   ga, kb, kt, r_s, lt_s, u_s, z_s,
                   a_sem, p_sem, ps_send, pp_send, p_recv, g_send, g_recv, h_send, h_recv,
                   gp_send, gp_recv, ga_send, ga_recv, a1_send, a1_recv, pr_send, pr_recv,
-                  rs_send, rs_recv, wd_send, wp_send, w_recv):
+                  rs_send, rs_recv, wd_send, wp_send, w_recv, re_send, half_recv):
     r = lax.axis_index("prow")
     q = lax.axis_index("pcol")
     z, core = lax.div(r, 2), lax.rem(r, 2)
@@ -160,8 +162,11 @@
     def greet_row(d):
         pl.semaphore_signal(barrier, inc=1, device_id={"prow": lax.rem(r + d, NP)}, device_id_type=pl.DeviceIdType.MESH)
 
+    def across_plane(d):
+        return lax.rem(lax.div(q, 4) + d // 4, 4) * 4 + lax.rem(lax.rem(q, 4) + d % 4, 4)
+
     def greet_col(d):
-        pl.semaphore_signal(barrier, inc=1, device_id={"pcol": lax.rem(q + d, NQ)}, device_id_type=pl.DeviceIdType.MESH)
+        pl.semaphore_signal(barrier, inc=1, device_id={"pcol": across_plane(d)}, device_id_type=pl.DeviceIdType.MESH)
 
     def load_panel():
         return pltpu.make_async_copy(a_hbm.at[:, pl.ds(0, B)], p_v, p_sem)
@@ -174,8 +179,10 @@
     def _():
         load_panel().start()
 
-    each(NQ, greet_col, 1)
-    each(NP, greet_row, 1)
+    for d in FAR_COLS:
+        greet_col(d)
+    for d in FAR_ROWS:
+        greet_row(d)
     each(TURNS, lambda j: load(j).start())
     pl.semaphore_wait(barrier, NP + NQ - 2)
 
@@ -216,10 +223,11 @@
     @pl.when(first_col)
     def _():
         load_panel().wait()
-        each(NQ, lambda j: scatter(j).start(), 1)
-        each(NQ, lambda j: spread(0, j).start(), 1)
+        for j in FAR_COLS:
+            scatter(j).start()
         gl[...] = dot3(p_v[...], p_v[...], ((0,), (0,)))
-        each(NP, lambda d: give_gram(lax.rem(r + d, NP)).start(), 1)
+        for d in FAR_ROWS:
+            give_gram(lax.rem(r + d, NP)).start()
         gbuf[pl.ds(r, 1)] = gl[pl.ds(pl.multiple_of(r * NB, NB), NB), :][None]
 
         @pl.when(first_row)
@@ -231,14 +239,12 @@
     def _():
         scatter(q).wait_recv()
 
-        def pass_on(d):
-            j = lax.rem(q + d, NQ)
+        for d in FAR_COLS:
+            j = across_plane(d)
 
             @pl.when(j != 0)
             def _():
                 spread(q, j).start()
-
-        each(NQ, pass_on, 1)
 
     each(TURNS // 2, turn)
 
@@ -258,8 +264,12 @@
         for j in range(1, NP):
             total = total + gbuf[j]
         gp[pl.ds(r, 1), :NB, :] = total[None]
-        each(NQ, lambda j: plane(j).start(), 1)
-        each(NP, lambda d: column_gather(d).start(), 1)
+        for j in FAR_COLS:
+            plane(j).start()
+        for d in FAR_ROWS:
+            column_gather(d).start()
+        for j in FAR_COLS:
+            spread(0, j).start()
 
     def give_a1(j):
         return remote(a1t.at[pl.ds(pl.multiple_of(j * PIECE, NB), PIECE)], a1b, a1_send.at[j], a1_recv, prow=j)
@@ -272,7 +282,7 @@
         a1b[...] = a1t[:PIECE, :]
 
     def group(step):
-        return lax.rem(lax.div(q, GROUPS) + (0, 1, 3, 2)[step], GROUPS)
+        return lax.rem(lax.div(q, GROUPS) + (2, 1, 3, 0)[step], GROUPS)
 
     def arrive_group(step):
         @pl.when(jnp.logical_not(first_col))
@@ -306,7 +316,8 @@
     @pl.when(jnp.logical_not(first_col))
     def _():
         plane(q).wait_recv()
-        each(NP, lambda d: column_gather(d).start(), 1)
+        for d in FAR_ROWS:
+            column_gather(d).start()
 
     for step in range(GROUPS):
         inner(step)
@@ -380,7 +391,7 @@
         return wsend(2 * zz + core, wp_send.at[zz], other)
 
     wacross(z).start()
-    for d in (2, 6, 1, 7, 4, 3, 5):
+    for d in SENT:
         wout(d).start()
 
     t_out[...] = dot3(u_s[...], z_s[...], ((1,), (1,)))
@@ -401,6 +412,19 @@
             lanes = lax.broadcasted_iota(jnp.int32, (B, B), 1)
             v2[:B, :] = jnp.where(lanes >= rows, -r_s[...], lt_s[...].T)
 
+    halves = {2: pl.ds(0, PIECE // 2), 6: pl.ds(PIECE // 2, PIECE // 2)}
+
+    def relay(d, k):
+        o = 2 * ring(d) + core
+        if k == 0:
+            return wsend(o, re_send.at[d // 4], 2 * ring(7 if d == 2 else 1) + core)
+        ref = wt.at[o, halves[d]]
+        return remote(ref, ref, re_send.at[2 + d // 4], half_recv.at[d // 4], prow=2 * ring(8 - d) + core)
+
+    def half_in(d):
+        ref = wt.at[2 * ring(4) + core, halves[d]]
+        return remote(ref, ref, re_send.at[2 + d // 4], half_recv.at[d // 4], prow=other)
+
     def come(o):
         wsend(o, wp_send.at[0], other).wait_recv()
 
@@ -422,14 +446,21 @@
     half, odd = lax.div(z, 2), lax.rem(z, 2)
     inner_group = lax.rem(half + 3 + 2 * odd, GROUPS)
     outer_group = lax.rem(half + 1 + 2 * odd, GROUPS)
-    for d in (1, 7, 2, 6):
+    for d in (2, 6):
+        come(2 * ring(d) + core)
+        relay(d, 0).start()
+        relay(d, 1).start()
+        wacross(ring(d)).start()
+    for d in (1, 7):
         come_and_pass(d)
     update(half)
     update(inner_group)
     for d in (3, 5):
         come_and_pass(d)
+    for d in (2, 6):
+        half_in(d).wait_recv()
+    wacross(ring(4)).start()
     update(outer_group)
-    come_and_pass(4)
     update(lax.rem(half + 2, GROUPS))
 
     @pl.when(first_col)
@@ -466,7 +497,11 @@
     each(NZ, lambda to: swap(to).wait_send())
     for d in FAR:
         reduce_to(ring(d)).wait_send()
+    for d in SENT:
         wout(d).wait_send()
+    for d in (2, 6):
+        relay(d, 0).wait_send()
+        relay(d, 1).wait_send()
     each(NZ, lambda zz: wacross(zz).wait_send())
 
 
@@ -488,7 +523,7 @@
             vm((B, 2 * B), F32), vm((B, 2 * B), F32), square, square, square, square, square,
             sem((TURNS,)), sem, sem((NQ,)), sem((NQ,)), sem((NQ,)), sem((NP,)), sem((NP,)),
             sem((NP,)), sem, sem((NQ,)), sem, sem((NP,)), sem((NP,)), sem((NP,)), sem, sem((NZ,)), sem((NZ,)),
-            sem((NZ,)), sem((NZ,)), sem((NZ,)), sem((NZ,)), sem((NP,)),
+            sem((NZ,)), sem((NZ,)), sem((NZ,)), sem((NZ,)), sem((NP,)), sem((4,)), sem((2,)),
         ],
         compiler_params=pltpu.CompilerParams(collective_id=0, has_side_effects=True, vmem_limit_bytes=40 * 2**20),
     )(pltpu.with_memory_space_constraint(matrix, pltpu.HBM))

time: 59.9 us -> 54.3 us (0.907)
  the two profiles are of different devices: /device:TPU:61 before, /device:TPU:25 now
where the time goes in v3:
time: 54.3 us; the launch traced here: 54.1 us
  Pallas kernels  53.5 us (99%)
  between operations  0.64 us (1%)
    pallas_call x1, Pallas kernels, factor_call(): pl.pallas_call(factor_kernel, out_shape=[vm((ROWS_L, COLS_L), F32), vm((B...  50.7 us
    pallas_call x1, Pallas kernels, store_call(): pl.pallas_call(store_kernel, out_shape=[pltpu.HBM(x.shape, F32), pltpu.HB...  2.77 us

profile of v3, /device:TPU:25, one launch (start us, length us, event | category | flops | bytes accessed | tf_op | source)
XLA Modules:
  0.0 54.1 jit_solution(10337152963651730664)
XLA Ops:
  0.6 50.7 %shard_map.30 = (f32[1024,1536]{1,0:T(8,128)S(1)}, f32[128,128]{1,0:T(8,128)S(1)}) custom-call(f32[1024,1536]{1,0:T(8,128)} %a_hbm.1), custom_call_target="tpu_custom_call" | custom-call | tf_op jit(solution)/shard_map/pallas_call | solution.py:512
  51.4 2.8 %shard_map.31 = (f32[1024,1536]{1,0:T(8,128)}, f32[128,128]{1,0:T(8,128)}) custom-call(f32[1024,1536]{1,0:T(8,128)S(1)} %get-tuple-element.4.x, f32[128,128]{1,0:T(8,128)S(1)} %get-tuple-element.5.t), custom_call_target="tpu_custom_call" | custom-call | tf_op jit(solution)/shard_map/pallas_call | solution.py:547

commit v4 on v3

--- a/solution.py
+++ b/solution.py
@@ -139,8 +139,9 @@
 
 GROUPS = 4
 GROUP = ROWS_L // GROUPS
-FAR = (4, 3, 5, 2, 6, 1, 7)
 SENT = (2, 6, 1, 7)
+SUM_ORDER = (3, 5, 4, 1, 7, 2, 6, 0)
+SUMMED = (4, 2, 6, 1, 7)
 FAR_ROWS = (8, 9, 7, 10, 6, 11, 5, 12, 4, 13, 3, 14, 2, 15, 1)
 FAR_COLS = (10, 9, 11, 8, 6, 14, 5, 7, 13, 15, 4, 12, 2, 1, 3)
 
@@ -150,7 +151,8 @@
                   ga, kb, kt, r_s, lt_s, u_s, z_s,
                   a_sem, p_sem, ps_send, pp_send, p_recv, g_send, g_recv, h_send, h_recv,
                   gp_send, gp_recv, ga_send, ga_recv, a1_send, a1_recv, pr_send, pr_recv,
-                  rs_send, rs_recv, wd_send, wp_send, w_recv, re_send, half_recv):
+                  rs_send, rs_recv, wd_send, wp_send, w_recv, re_send, half_recv,
+                  lent, le_send, le_recv):
     r = lax.axis_index("prow")
     q = lax.axis_index("pcol")
     z, core = lax.div(r, 2), lax.rem(r, 2)
@@ -332,20 +334,27 @@
     def reduce_to(to):
         return remote(pair.at[to], rsb.at[z], rs_send.at[to], rs_recv.at[z], prow=2 * to + core)
 
-    def far(d):
-        return ring(jnp.where(d == NZ - 1, NZ, NZ // 2 + jnp.where(lax.rem(d, 2) == 0, 1, -1) * lax.div(d + 1, 2)))
-
-    def ours_step(d):
-        to = far(d)
+    def lean(d):
+        k = d // 4
+        return remote(pair.at[ring(d)], lent.at[k], le_send.at[k], le_recv.at[k],
+                      prow=2 * ring(1 if d == 3 else 7) + core)
+
+    for d in SUM_ORDER:
+        swap(ring(d)).start()
+    for d in SUM_ORDER:
+        to = ring(d)
         swap(to).wait_recv()
         pair[pl.ds(to, 1)] += ct[pl.ds(pl.multiple_of((2 * to + core) * PIECE, 32), PIECE), :][None]
-
-        @pl.when(to != z)
-        def _():
+        if d in (3, 5):
+            lean(d).start()
+        elif d in (4, 1, 7):
             reduce_to(to).start()
 
-    each(NZ, lambda d: swap(far(d)).start())
-    each(NZ, ours_step)
+    def send_on():
+        for d, k in ((2, 3), (6, 5)):
+            lean(k).wait_recv()
+            pair[pl.ds(ring(d), 1)] += lent[pl.ds(k // 4, 1)]
+            reduce_to(ring(d)).start()
 
     def arrive_gram(d):
         j = lax.rem(r + d, NP)
@@ -366,7 +375,9 @@
         lu_block(k0, *state, kb, kt, lt_s, u_s, z_s)
         return chol_block(pl.multiple_of(k0 + NB, NB), ga, r_s)
 
-    state = lax.fori_loop(0, B // NB - 1, step, state)
+    state = lax.fori_loop(0, 7, step, state)
+    send_on()
+    state = lax.fori_loop(7, B // NB - 1, step, state)
     lu_block(B - NB, *state, kb, kt, lt_s, u_s, z_s)
 
     @pl.when(jnp.logical_not(first_row))
@@ -375,9 +386,9 @@
 
     m = kb[:, B:]
     total = pair[pl.ds(z, 1)][0] + dot3(a1b[...], r_s[...], ((1,), (0,)))
-    for d in FAR:
+    for d in SUMMED:
         remote(rsb.at[ring(d)], rsb.at[ring(d)], rs_send.at[ring(d)], rs_recv.at[ring(d)], prow=r).wait_recv()
-    for d in FAR:
+    for d in SUMMED:
         total = total + rsb[pl.ds(ring(d), 1)][0]
     wt[pl.ds(r, 1)] = dot3(total, m, ((1,), (1,)))[None]
 
@@ -495,8 +506,10 @@
 
     each(NP, lambda d: column_gather(d).wait_send(), 1)
     each(NZ, lambda to: swap(to).wait_send())
-    for d in FAR:
+    for d in SUMMED:
         reduce_to(ring(d)).wait_send()
+    for d in (3, 5):
+        lean(d).wait_send()
     for d in SENT:
         wout(d).wait_send()
     for d in (2, 6):
@@ -524,6 +537,7 @@
             sem((TURNS,)), sem, sem((NQ,)), sem((NQ,)), sem((NQ,)), sem((NP,)), sem((NP,)),
             sem((NP,)), sem, sem((NQ,)), sem, sem((NP,)), sem((NP,)), sem((NP,)), sem, sem((NZ,)), sem((NZ,)),
             sem((NZ,)), sem((NZ,)), sem((NZ,)), sem((NZ,)), sem((NP,)), sem((4,)), sem((2,)),
+            vm((2, PIECE, B), F32), sem((2,)), sem((2,)),
         ],
         compiler_params=pltpu.CompilerParams(collective_id=0, has_side_effects=True, vmem_limit_bytes=40 * 2**20),
     )(pltpu.with_memory_space_constraint(matrix, pltpu.HBM))

time: 54.3 us -> 53.2 us (0.980)
  Pallas kernels: 53.5 us -> 52.5 us
    pallas_call x1, Pallas kernels: 50.7 us -> 49.7 us  [factor_call(): pl.pallas_call(factor_kernel, out_shape=[vm((ROWS_L, COLS_L), F32), vm((B...]
where the time goes in v4:
time: 53.2 us
  Pallas kernels  52.5 us (99%)
  between operations  0.64 us (1%)
    pallas_call x1, Pallas kernels, factor_call(): pl.pallas_call(factor_kernel, out_shape=[vm((ROWS_L, COLS_L), F32), vm((B...  49.7 us
    pallas_call x1, Pallas kernels, store_call(): pl.pallas_call(store_kernel, out_shape=[pltpu.HBM(x.shape, F32), pltpu.HB...  2.77 us

profile of v4, /device:TPU:25, one launch (start us, length us, event | category | flops | bytes accessed | tf_op | source)
XLA Modules:
  0.0 53.2 jit_solution(12893170698927389689)
XLA Ops:
  0.6 49.7 %shard_map.30 = (f32[1024,1536]{1,0:T(8,128)S(1)}, f32[128,128]{1,0:T(8,128)S(1)}) custom-call(f32[1024,1536]{1,0:T(8,128)} %a_hbm.1), custom_call_target="tpu_custom_call" | custom-call | tf_op jit(solution)/shard_map/pallas_call | solution.py:525
  50.4 2.8 %shard_map.31 = (f32[1024,1536]{1,0:T(8,128)}, f32[128,128]{1,0:T(8,128)}) custom-call(f32[1024,1536]{1,0:T(8,128)S(1)} %get-tuple-element.4.x, f32[128,128]{1,0:T(8,128)S(1)} %get-tuple-element.5.t), custom_call_target="tpu_custom_call" | custom-call | tf_op jit(solution)/shard_map/pallas_call | solution.py:561

commit v5 on v4

--- a/solution.py
+++ b/solution.py
@@ -170,8 +170,9 @@
     def greet_col(d):
         pl.semaphore_signal(barrier, inc=1, device_id={"pcol": across_plane(d)}, device_id_type=pl.DeviceIdType.MESH)
 
-    def load_panel():
-        return pltpu.make_async_copy(a_hbm.at[:, pl.ds(0, B)], p_v, p_sem)
+    def load_panel(g):
+        at = pl.ds(g * GROUP, GROUP)
+        return pltpu.make_async_copy(a_hbm.at[at, pl.ds(0, B)], p_v.at[at], p_sem.at[g])
 
     def load(j):
         at = pl.ds(pl.multiple_of(j * B, B), B)
@@ -179,7 +180,8 @@
 
     @pl.when(first_col)
     def _():
-        load_panel().start()
+        for g in (2, 1, 3, 0):
+            load_panel(g).start()
 
     for d in FAR_COLS:
         greet_col(d)
@@ -224,8 +226,11 @@
 
     @pl.when(first_col)
     def _():
-        load_panel().wait()
+        waited = set()
         for j in FAR_COLS:
+            if j // GROUPS not in waited:
+                load_panel(j // GROUPS).wait()
+                waited.add(j // GROUPS)
             scatter(j).start()
         gl[...] = dot3(p_v[...], p_v[...], ((0,), (0,)))
         for d in FAR_ROWS:
@@ -534,7 +539,7 @@
             vm((NP, NB, B), F32), vm((NP, 2 * NB, B), F32), vm((NP, PIECE, B), F32), vm((ROWS_L, 3 * B), BF16),
             vm((ROWS_L, B), F32),
             vm((B, 2 * B), F32), vm((B, 2 * B), F32), square, square, square, square, square,
-            sem((TURNS,)), sem, sem((NQ,)), sem((NQ,)), sem((NQ,)), sem((NP,)), sem((NP,)),
+            sem((TURNS,)), sem((GROUPS,)), sem((NQ,)), sem((NQ,)), sem((NQ,)), sem((NP,)), sem((NP,)),
             sem((NP,)), sem, sem((NQ,)), sem, sem((NP,)), sem((NP,)), sem((NP,)), sem, sem((NZ,)), sem((NZ,)),
             sem((NZ,)), sem((NZ,)), sem((NZ,)), sem((NZ,)), sem((NP,)), sem((4,)), sem((2,)),
             vm((2, PIECE, B), F32), sem((2,)), sem((2,)),

time: 53.2 us -> 53.2 us (level)
  no operation moved by 1% of the time
where the time goes in v5:
time: 53.2 us; the launch traced here: 53.1 us
  Pallas kernels  52.5 us (99%)
  between operations  0.64 us (1%)
    pallas_call x1, Pallas kernels, factor_call(): pl.pallas_call(factor_kernel, out_shape=[vm((ROWS_L, COLS_L), F32), vm((B...  49.7 us
    pallas_call x1, Pallas kernels, store_call(): pl.pallas_call(store_kernel, out_shape=[pltpu.HBM(x.shape, F32), pltpu.HB...  2.77 us

profile of v5, /device:TPU:25, one launch (start us, length us, event | category | flops | bytes accessed | tf_op | source)
XLA Modules:
  0.0 53.1 jit_solution(6548772758686941594)
XLA Ops:
  0.6 49.7 %shard_map.30 = (f32[1024,1536]{1,0:T(8,128)S(1)}, f32[128,128]{1,0:T(8,128)S(1)}) custom-call(f32[1024,1536]{1,0:T(8,128)} %a_hbm.1), custom_call_target="tpu_custom_call" | custom-call | tf_op jit(solution)/shard_map/pallas_call | solution.py:530
  50.4 2.8 %shard_map.31 = (f32[1024,1536]{1,0:T(8,128)}, f32[128,128]{1,0:T(8,128)}) custom-call(f32[1024,1536]{1,0:T(8,128)S(1)} %get-tuple-element.4.x, f32[128,128]{1,0:T(8,128)S(1)} %get-tuple-element.5.t), custom_call_target="tpu_custom_call" | custom-call | tf_op jit(solution)/shard_map/pallas_call | solution.py:566
